TPU v7x, 32 devices: a whole 2x2x4 slice. The times are simulated.
32 devices in a mesh: dp: 4 (over z), mp: 8 (over y, x, core).
Axes of the slice: x: 2, y: 2, z: 4, core: 2. Of those that a mesh axis runs over, the one named last changes fastest.
Arguments:
- gradient: bfloat16 [4608, 36864], P('dp', 'mp'), may hold values from -14 to 14
- sketches: bfloat16 [1024, 36864], P('dp', 'mp'), may hold values from -4.5 to 4.5
- start_basis: float32 [512, 256], replicated, may hold values from -6 to 6
Outputs:
- preconditioned: bfloat16 [4608, 36864], P('dp', 'mp')
All inputs are finite; a program needn't handle non-finite values.
Results may differ from a plain program's by a relative error of at most 0.0065.
Values may be sent and summed in bfloat16 or wider, within the bound.
A program may use at most 128 MiB of HBM per device.

v0:
```python
import jax
import jax.numpy as jnp
from jax import lax
from jax.sharding import PartitionSpec as P

K = 256
ITERS = 4
NS_STEPS = 6


def partner_2(value, axis, bit):
    mask = 2**bit
    pairs = [(source, source ^ mask) for source in range(lax.axis_size(axis))]
    return lax.ppermute(value, axis, pairs)


def orthonormalize(image):
    scaled = image / jnp.sqrt(jnp.sum(image * image) + 1e-06)
    for inner_step in range(NS_STEPS):
        square = jnp.dot(scaled.T, scaled, precision=lax.Precision.HIGHEST)
        scaled = 1.5 * scaled - 0.5 * jnp.dot(scaled, square, precision=lax.Precision.HIGHEST)
    return scaled


def finish_merge(gram, stacked, start_basis):
    basis = start_basis
    for step in range(ITERS):
        image = jnp.dot(gram, basis, precision=lax.Precision.HIGHEST)
        basis = orthonormalize(image)
    energy = jnp.sum(basis * jnp.dot(gram, basis, precision=lax.Precision.HIGHEST), axis=0)
    shrink = 0.5 * jnp.min(energy)
    factor = jnp.sqrt(1.0 - shrink / energy)
    weights = (factor[:, None] * basis.T).astype(jnp.bfloat16)
    return jnp.dot(weights, stacked, preferred_element_type=jnp.float32).astype(jnp.bfloat16)


def solve_rows(proj, sketch_gram):
    rho = jnp.trace(sketch_gram) / K
    system = sketch_gram + rho * jnp.eye(K, dtype=jnp.float32)
    lower = jnp.linalg.cholesky(system)
    halfway = lax.linalg.triangular_solve(
        lower, proj, left_side=False, lower=True, transpose_a=True
    )
    solved = lax.linalg.triangular_solve(
        lower, halfway, left_side=False, lower=True, transpose_a=False
    )
    return solved.astype(jnp.bfloat16)


def local(gradient, sketches, start_basis):
    levels = lax.axis_size("dp").bit_length() - 1
    position = lax.axis_index("dp")
    current = sketches
    for level in range(levels):
        partner = partner_2(current, "dp", level)
        upper_side = position >> level & 1 == 1
        stacked = jnp.where(
            upper_side,
            jnp.concatenate([partner, current], axis=0),
            jnp.concatenate([current, partner], axis=0),
        )
        local_gram = jnp.dot(stacked, stacked.T, preferred_element_type=jnp.float32)
        gram = lax.psum(local_gram.astype(jnp.bfloat16), "mp").astype(jnp.float32)
        current = finish_merge(gram, stacked, start_basis)
    local_proj = jnp.dot(gradient, current.T, preferred_element_type=jnp.float32)
    local_gram = jnp.dot(current, current.T, preferred_element_type=jnp.float32)
    proj, sketch_gram = (
        lax.psum(local_proj.astype(jnp.bfloat16), "mp").astype(jnp.float32),
        lax.psum(local_gram.astype(jnp.bfloat16), "mp").astype(jnp.float32),
    )
    solved = solve_rows(proj, sketch_gram)
    result = gradient.astype(jnp.float32) - jnp.dot(
        solved, current, preferred_element_type=jnp.float32
    )
    return result.astype(jnp.bfloat16)


def solution(mesh):
    in_specs = (P("dp", "mp"), P("dp", "mp"), P())
    out_specs = P("dp", "mp")
    return jax.shard_map(local, mesh=mesh, in_specs=in_specs, out_specs=out_specs, check_vma=False)
```

profile of v0, /device:TPU:25, one launch (start us, length us, event | category | flops | bytes accessed | tf_op | source)
XLA Modules:
  0.0 549.7 jit_solution(5503303964622626691)
XLA Ops:
  6.7 52.2 %collective-permute-done = bf16[256,4608]{1,0:T(8,128)(2,1)S(1)} collective-permute-done((bf16[256,4608]{1,0:T(8,128)(2,1)}, bf16[256,4608]{1,0:T(8,128)(2,1)S(1)}, u32[]{:S(2)}, u32[]{:S(2)}) %collective-permute-start) | collective-permute-done | bytes 2359328 | tf_op jit(solution)/shard_map/ppermute | solution.py:14
  58.9 8.1 %convolution_convert_fusion.5 = bf16[512,512]{1,0:T(8,128)(2,1)} fusion(bf16[256,4608]{1,0:T(8,128)(2,1)} %param.4, bf16[256,4608]{1,0:T(8,128)(2,1)S(1)} %collective-permute-done, pred[]{:T(512)S(6)} %eq.14), kind=kOutput, calls=%fused_computation.14 | convolution fusion | flops 2437414912 | bytes 5242881 | tf_op jit(solution)/shard_map/dot_general | solution.py:62
  67.2 55.3 %all-reduce.6.cloned.1.call-done = bf16[512,512]{1,0:T(8,128)(2,1)} async-done(((bf16[512,512]{1,0:T(8,128)(2,1)}), bf16[512,512]{1,0:T(8,128)(2,1)}) %all-reduce.6.cloned.1.call-update) | async-done | bytes 524304 | tf_op jit(solution)/shard_map/psum | solution.py:63
  122.5 2.4 multiply_reduce_fusion.7
  135.5 1.3 multiply_reduce_fusion.6
  147.6 1.3 multiply_reduce_fusion.5
  152.9 1.4 fusion.94
  159.9 1.3 multiply_reduce_fusion.4
  174.0 6.7 %convolution_convert_fusion.1 = bf16[256,4608]{1,0:T(8,128)(2,1)} fusion(bf16[256,4608]{1,0:T(8,128)(2,1)} %param.4, bf16[256,4608]{1,0:T(8,128)(2,1)} %copy-done.7, pred[]{:T(512)S(6)} %eq.14, f32[512,256]{1,0:T(8,128)S(1)} %fusion.26, f32[256]{0:T(256)S(1)} %subtract_sqrt_fusion.1), kind=kOutput, calls=%fused_computation.5 | convolution fusion | flops 1230635008 | bytes 7603201 | tf_op jit(solution)/shard_map/dot_general | solution.py:34
  180.9 104.6 %collective-permute-done.1 = bf16[256,4608]{1,0:T(8,128)(2,1)S(1)} collective-permute-done((bf16[256,4608]{1,0:T(8,128)(2,1)}, bf16[256,4608]{1,0:T(8,128)(2,1)S(1)}, u32[]{:S(2)}, u32[]{:S(2)}) %collective-permute-start.1) | collective-permute-done | bytes 2359328 | tf_op jit(solution)/shard_map/ppermute | solution.py:14
  285.5 8.1 %convolution_convert_fusion.4 = bf16[512,512]{1,0:T(8,128)(2,1)} fusion(bf16[256,4608]{1,0:T(8,128)(2,1)} %convolution_convert_fusion.1, bf16[256,4608]{1,0:T(8,128)(2,1)S(1)} %collective-permute-done.1, pred[]{:T(512)S(6)} %eq.13), kind=kOutput, calls=%fused_computation.13 | convolution fusion | flops 2437414912 | bytes 5242881 | tf_op jit(solution)/shard_map/dot_general | solution.py:62
  293.9 52.7 %all-reduce.8.cloned.1.call-done = bf16[512,512]{1,0:T(8,128)(2,1)} async-done(((bf16[512,512]{1,0:T(8,128)(2,1)}), bf16[512,512]{1,0:T(8,128)(2,1)}) %all-reduce.8.cloned.1.call-update) | async-done | bytes 524304 | tf_op jit(solution)/shard_map/psum | solution.py:63
  346.6 2.4 multiply_reduce_fusion.3
  397.2 5.4 convolution_convert_fusion
  402.6 1.5 convolution_convert_fusion.6
  404.1 4.0 fusion.1
  408.2 54.9 %all-reduce.10.cloned.1.call-done = (bf16[1152,256]{0,1:T(8,128)(2,1)}, bf16[256,256]{0,1:T(8,128)(2,1)}) async-done(((bf16[1152,256]{0,1:T(8,128)(2,1)}, bf16[256,256]{0,1:T(8,128)(2,1)}), (bf16[1152,256]{0,1:T(8,128)(2,1)}, bf16[256,256]{0,1:T(8,128)(2,1)})) %all-reduce.10.cloned.1.call-update) | async-done | bytes 720912 | tf_op jit(solution)/shard_map/psum | solution.py:68
  463.1 1.6 fusion.57
  467.3 12.1 %cholesky.49 = f32[128,128]{1,0:T(8,128)S(1)} custom-call(f32[128,128]{1,0:T(8,128)S(1)} %cholesky.115), custom_call_target="Cholesky" | custom-call | tf_op jit(solution)/shard_map/jit(cholesky)/cholesky | solution.py:40
  479.6 9.8 %custom-call.16 = f32[1,128,128]{1,2,0:T(8,128)S(1)} custom-call(f32[1,128,128]{2,1,0:T(8,128)S(1)} %get-tuple-element.30), custom_call_target="InvertDiagBlocksLowerTriangular" | custom-call | tf_op jit(solution)/shard_map/jit(cholesky)/cholesky | solution.py:40
  490.0 11.7 %cholesky.103 = f32[128,128]{1,0:T(8,128)S(1)} custom-call(f32[128,128]{1,0:T(8,128)S(1)} %convolution_subtract_fusion.3), custom_call_target="Cholesky" | custom-call | tf_op jit(solution)/shard_map/jit(cholesky)/cholesky | solution.py:40
  503.9 5.4 while.1
  509.4 20.5 %custom-call.17 = f32[2,128,128]{1,2,0:T(8,128)S(1)} custom-call(f32[2,128,128]{2,1,0:T(8,128)} %get-tuple-element.12), custom_call_target="InvertDiagBlocksLowerTriangular" | custom-call | tf_op jit(solution)/shard_map/triangular_solve | solution.py:41
  534.7 8.3 %fusion = bf16[1152,4608]{1,0:T(8,128)(2,1)} fusion(bf16[256,4608]{1,0:T(8,128)(2,1)S(1)} %copy-done.5, bf16[1152,4608]{1,0:T(8,128)(2,1)} %param.3, bf16[1152,128]{0,1:T(8,128)(2,1)S(1)} %get-tuple-element.47, bf16[1152,128]{0,1:T(8,128)(2,1)S(1)} %convolution_convert_fusion.3), kind=kOutput, calls=%fused_computation.3 | convolution fusion | flops 2735013888 | bytes 24182784 | tf_op jit(solution)/shard_map/dot_general | solution.py:72
  (172 shorter events, 99.0 us)
Async XLA Ops:
  6.5 116.0 %copy-start = (f32[512,256]{1,0:T(8,128)S(1)}, f32[512,256]{1,0:T(8,128)}, u32[]{:S(2)}) copy-start(f32[512,256]{1,0:T(8,128)} %param.5) | copy-start | bytes 1572868
  6.5 116.0 %all-reduce.6.cloned.1.call-start = ((), (), s32[]{:S(2)}) async-start(), calls=%async_computation | async-start | bytes 1048576 | tf_op jit(solution)/shard_map/psum | solution.py:63
  6.5 52.3 %collective-permute-start = (bf16[256,4608]{1,0:T(8,128)(2,1)}, bf16[256,4608]{1,0:T(8,128)(2,1)S(1)}, u32[]{:S(2)}, u32[]{:S(2)}) collective-permute-start(bf16[256,4608]{1,0:T(8,128)(2,1)} %param.4), channel_id=1, source_target_pairs={{0,8},{8,0},{16,24},{24,16},{1,9},{9,1},{17,25},{25,17},{2,10},{10... | collective-permute-start | bytes 7077896 | tf_op jit(solution)/shard_map/ppermute | solution.py:14
  58.9 8.1 %copy-start.7 = (bf16[256,4608]{1,0:T(8,128)(2,1)}, bf16[256,4608]{1,0:T(8,128)(2,1)S(1)}, u32[]{:S(2)}) copy-start(bf16[256,4608]{1,0:T(8,128)(2,1)S(1)} %collective-permute-done) | copy-start | bytes 7077892
  66.9 279.6 %all-reduce.8.cloned.1.call-start = ((), (), s32[]{:S(2)}) async-start(), calls=%async_computation.1 | async-start | bytes 1048576 | tf_op jit(solution)/shard_map/psum | solution.py:63
  129.9 5.5 %copy-start.3 = (bf16[512,512]{1,0:T(8,128)(2,1)S(1)}, bf16[512,512]{1,0:T(8,128)(2,1)}, u32[]{:S(2)}) copy-start(bf16[512,512]{1,0:T(8,128)(2,1)} %all-reduce.6.cloned.1.call-done) | copy-start | bytes 1572868
  180.7 104.8 %collective-permute-start.1 = (bf16[256,4608]{1,0:T(8,128)(2,1)}, bf16[256,4608]{1,0:T(8,128)(2,1)S(1)}, u32[]{:S(2)}, u32[]{:S(2)}) collective-permute-start(bf16[256,4608]{1,0:T(8,128)(2,1)} %convolution_convert_fusion.1), channel_id=1, source_target_pairs={{0,16},{8,24},{16,0},{24,8},{1,17},{9,25},{17,1},{25,9},{2,18},{10... | collective-permute-start | bytes 7077896 | tf_op jit(solution)/shard_map/ppermute | solution.py:14
  285.5 8.1 %copy-start.8 = (bf16[256,4608]{1,0:T(8,128)(2,1)}, bf16[256,4608]{1,0:T(8,128)(2,1)S(1)}, u32[]{:S(2)}) copy-start(bf16[256,4608]{1,0:T(8,128)(2,1)S(1)} %collective-permute-done.1) | copy-start | bytes 7077892
  293.6 169.5 %all-reduce.10.cloned.1.call-start = ((), (), s32[]{:S(2)}) async-start(), calls=%async_computation.2 | async-start | bytes 1441792 | tf_op jit(solution)/shard_map/psum | solution.py:68
  353.9 5.5 %copy-start.2 = (bf16[512,512]{1,0:T(8,128)(2,1)S(1)}, bf16[512,512]{1,0:T(8,128)(2,1)}, u32[]{:S(2)}) copy-start(bf16[512,512]{1,0:T(8,128)(2,1)} %all-reduce.8.cloned.1.call-done) | copy-start | bytes 1572868
  393.6 10.5 %slice-start = ((s8[10616832]{0:T(1024)(128)(4,1)}), s8[2228224]{0:T(1024)(128)(4,1)S(1)}, s32[]{:S(2)}) async-start(s8[10616832]{0:T(1024)(128)(4,1)} %bitcast.231), calls=%async_computation.3 | async-start | bytes 4456448
  397.1 7.0 %slice-start.1 = ((s8[10616832]{0:T(1024)(128)(4,1)}), s8[4194304]{0:T(1024)(128)(4,1)S(1)}, s32[]{:S(2)}) async-start(s8[10616832]{0:T(1024)(128)(4,1)} %bitcast.231), calls=%async_computation.4 | async-start | bytes 8388608
  397.1 7.0 %slice-start.2 = ((s8[10616832]{0:T(1024)(128)(4,1)}), s8[4194304]{0:T(1024)(128)(4,1)S(1)}, s32[]{:S(2)}) async-start(s8[10616832]{0:T(1024)(128)(4,1)} %bitcast.231), calls=%async_computation.5 | async-start | bytes 8388608
  402.6 1.5 copy-start.4
  463.1 66.7 %copy-start.6 = (bf16[1152,256]{0,1:T(8,128)(2,1)S(1)}, bf16[1152,256]{0,1:T(8,128)(2,1)}, u32[]{:S(2)}) copy-start(bf16[1152,256]{0,1:T(8,128)(2,1)} %get-tuple-element.25) | copy-start | bytes 1769476
  503.9 30.8 %copy-start.5 = (bf16[256,4608]{1,0:T(8,128)(2,1)S(1)}, bf16[256,4608]{1,0:T(8,128)(2,1)}, u32[]{:S(2)}) copy-start(bf16[256,4608]{1,0:T(8,128)(2,1)} %copy-done.4) | copy-start | bytes 7077892
  534.7 8.3 %copy-start.1 = (f32[512,256]{1,0:T(8,128)S(1)}, f32[512,256]{1,0:T(8,128)}, u32[]{:S(2)}) copy-start(f32[512,256]{1,0:T(8,128)} %param.5) | copy-start | bytes 1572868
Sparse Core Ops, SparseCore 0:
  67.1 55.3 all-reduce.5
  293.7 52.8 all-reduce.7
  408.3 54.7 all-reduce.9
where the time goes:
time: 556 us; the launch traced here: 550 us
  waiting for transfers between devices  320 us (58%)
  matrix products  141 us (25%)
  other arithmetic  59.7 us (11%)
  between operations  22.9 us (4%)
  local copies, waits for them, and re-layouts  5.82 us (1%)
    ppermute x2, waiting for transfers between devices, partner_2(): return lax.ppermute(value, axis, pairs)  157 us
    psum x2, waiting for transfers between devices, local(): gram = lax.psum(local_gram.astype(jnp.bfloat16), 'mp').astype(jnp.float32)  108 us
    psum x1, waiting for transfers between devices, local(): lax.psum(local_proj.astype(jnp.bfloat16), 'mp').astype(jnp.float32)  54.9 us
    dot_general x48, matrix products, orthonormalize(): square = jnp.dot(scaled.T, scaled, precision=lax.Precision.HIGHEST)  50.7 us
    another operation x6, other arithmetic, solve_rows(): lower = jnp.linalg.cholesky(system)  34.4 us
    dot_general x48, matrix products, orthonormalize(): jnp.dot(scaled, square, precision=lax.Precision.HIGHEST)  28.6 us
    another operation x3, other arithmetic, solve_rows(): lax.linalg.triangular_solve(lower, proj, left_side=False, lower=True, tra...  20.5 us
    dot_general x2, matrix products, local(): local_gram = jnp.dot(stacked, stacked.T, preferred_element_type=jnp.float32)  16.1 us
  transfers between devices with their start and end apart: 5, of which 5 were waited for; matrix products, arithmetic and copies ran while one was open for 0% of the time, Pallas kernels for 0%

commit v1 on v0

v1 whole, which is shorter than its diff:
```python
import functools
import jax
import jax.numpy as jnp
from jax import lax
from jax.experimental import pallas as pl
from jax.experimental.pallas import tpu as pltpu
from jax.sharding import PartitionSpec as P

K = 256
ITERS = 4
NS_STEPS = 6
INVERSE_STEPS = 11
BF16 = jnp.bfloat16
F32 = jnp.float32
MESH = pl.DeviceIdType.MESH
VMEM_LIMIT = 56 * 2**20
NN = (((1,), (0,)), ((), ()))
NT = (((1,), (1,)), ((), ()))


def peer(axis, offset):
    size = lax.axis_size(axis)
    return lax.rem(lax.axis_index(axis) + offset, size)


def greet(axes):
    barrier = pltpu.get_barrier_semaphore()
    count = 0
    for axis in axes:
        for offset in range(1, lax.axis_size(axis)):
            pl.semaphore_signal(
                barrier, inc=1, device_id={axis: peer(axis, offset)}, device_id_type=MESH
            )
            count += 1
    pl.semaphore_wait(barrier, count)


def send(axis, offset, source, target, send_sem, recv_sem):
    copy = pltpu.make_async_remote_copy(
        src_ref=source,
        dst_ref=target,
        send_sem=send_sem.at[offset - 1],
        recv_sem=recv_sem.at[offset - 1],
        device_id={axis: peer(axis, offset)},
        device_id_type=MESH,
    )
    copy.start()
    return copy


def rows_of(index, count):
    return pl.ds(pl.multiple_of(index * count, 16), count)


def columns_of(index, count):
    return pl.ds(pl.multiple_of(index * count, 128), count)


def dot(a, b, dims=NN):
    return lax.dot_general(a, b, dims, preferred_element_type=F32)


def split(x):
    high = x.astype(BF16)
    return high, (x - high.astype(F32)).astype(BF16)


def dot_split(a, b, dims=NN):
    return dot(a[0], b[0], dims) + (dot(a[0], b[1], dims) + dot(a[1], b[0], dims))


def sum_slots(ref):
    total = ref[0].astype(F32)
    for slot in range(1, ref.shape[0]):
        total = total + ref[slot].astype(F32)
    return total


def gram_kernel(
    n, mp, width, share, sketch_ref, slice_ref, gram_ref, part, mp_slots, dp_slots,
    local_sem, s0, r0, s1, r1, s2, r2, s3, r3,
):
    me_dp, me_mp = lax.axis_index("dp"), lax.axis_index("mp")
    own = pltpu.make_async_copy(
        sketch_ref.at[:, columns_of(me_dp, width)], slice_ref.at[rows_of(me_dp, K)], local_sem
    )
    own.start()
    greet(("dp", "mp"))
    copies = [
        send(
            "dp", d, sketch_ref.at[:, columns_of(peer("dp", d), width)],
            slice_ref.at[rows_of(me_dp, K)], s0, r0,
        )
        for d in range(1, n)
    ]
    own.wait()
    for copy in copies:
        copy.wait()
    block = 0
    for i in range(n):
        for j in range(i, n):
            part[block * K:(block + 1) * K, :] = dot(
                slice_ref[i * K:(i + 1) * K, :], slice_ref[j * K:(j + 1) * K, :], NT
            ).astype(BF16)
            block += 1
    copies = [
        send("mp", d, part.at[rows_of(peer("mp", d), share)], mp_slots.at[me_mp], s1, r1)
        for d in range(1, mp)
    ]
    mp_slots[me_mp] = part[rows_of(me_mp, share), :]
    for copy in copies:
        copy.wait()
    dp_slots[me_dp] = sum_slots(mp_slots).astype(BF16)
    copies = [
        send("dp", d, dp_slots.at[me_dp], dp_slots.at[me_dp], s2, r2) for d in range(1, n)
    ]
    for copy in copies:
        copy.wait()
    mine = gram_ref.at[rows_of(me_mp, share)]
    mine[...] = sum_slots(dp_slots).astype(BF16)
    copies = [send("mp", d, mine, mine, s3, r3) for d in range(1, mp)]
    for copy in copies:
        copy.wait()


def merge_kernel(n, gram_ref, basis_ref, weights_ref, system_ref, full, following, basis):
    block = 0
    for i in range(n):
        for j in range(i, n):
            value = gram_ref[block * K:(block + 1) * K, :].astype(F32)
            full[i * K:(i + 1) * K, j * K:(j + 1) * K] = value
            if j > i:
                full[j * K:(j + 1) * K, i * K:(i + 1) * K] = value.T
            block += 1
    source, target = full, following
    blocks, first = n, 0
    while blocks > 1:
        pairs = blocks // 2
        sides = [slice(2 * K * p, 2 * K * (p + 1)) for p in range(pairs)]
        for p in range(pairs):
            basis[p] = basis_ref[...]

        def newton_schulz(step, carry):
            for p in range(pairs):
                value = basis[p]
                parts = split(value)
                square = split(dot_split(parts, parts, NT))
                basis[p] = 1.5 * value - 0.5 * dot_split(square, parts)
            return carry

        def iteration(step, carry):
            for p in range(pairs):
                image = dot_split(split(basis[p]), split(source[sides[p], sides[p]]))
                basis[p] = image / jnp.sqrt(jnp.sum(image * image) + 1e-06)
            return lax.fori_loop(0, NS_STEPS, newton_schulz, carry)

        lax.fori_loop(0, ITERS, iteration, 0)
        for p in range(pairs):
            value = basis[p]
            image = dot_split(split(value), split(source[sides[p], sides[p]]))
            energy = jnp.sum(value * image, axis=1, keepdims=True)
            shrink = 0.5 * jnp.min(energy)
            factor = jnp.sqrt(1.0 - shrink / energy)
            weights_ref[first + p] = (factor * value).astype(BF16)
        for a in range(pairs):
            for b in range(a, pairs):
                high, low = split(source[sides[a], sides[b]])
                left = weights_ref[first + a]
                high, low = split(dot(left, high) + dot(left, low))
                right = weights_ref[first + b]
                value = dot(high, right, NT) + dot(low, right, NT)
                target[a * K:(a + 1) * K, b * K:(b + 1) * K] = value
                if b > a:
                    target[b * K:(b + 1) * K, a * K:(a + 1) * K] = value.T
        source, target = target, source
        first += pairs
        blocks = pairs
    system_ref[...] = source[:K, :K]


def invert(system_ref, inverse):
    row = lax.broadcasted_iota(jnp.int32, (K, K), 0)
    column = lax.broadcasted_iota(jnp.int32, (K, K), 1)
    eye = (row == column).astype(F32)
    gram = system_ref[...]
    rho = jnp.sum(gram * eye) / K
    system = gram + rho * eye
    row_sums = jnp.sum(jnp.abs(system), axis=1, keepdims=True)
    bound = jnp.minimum(jnp.max(row_sums), (K + 1) * rho)
    inverse[...] = eye * (2.0 / (bound + rho))
    parts = split(system)

    def step(index, carry):
        value = inverse[...]
        pieces = split(value)
        residual = 2.0 * eye - dot_split(parts, pieces)
        inverse[...] = dot_split(pieces, split(residual))
        return carry

    lax.fori_loop(0, INVERSE_STEPS, step, 0)


def solve_kernel(
    n, mp, width, share, rows, weights_ref, system_ref, slice_ref, gradient_ref,
    merged_ref, solved_ref, grad, level, inverse, proj, sums, mp_slots,
    local_sem, s0, r0, s1, r1, s2, r2,
):
    me_dp, me_mp = lax.axis_index("dp"), lax.axis_index("mp")
    load = pltpu.make_async_copy(gradient_ref, grad, local_sem)
    load.start()
    mine = merged_ref.at[:, columns_of(me_dp, width)]
    source, first, blocks = slice_ref, 0, n
    while blocks > 1:
        blocks //= 2
        for p in range(blocks):
            value = dot(weights_ref[first + p], source[2 * K * p:2 * K * (p + 1), :]).astype(BF16)
            if blocks == 1:
                mine[...] = value
            else:
                level[p * K:(p + 1) * K, :] = value
        source = level
        first += blocks
    greet(("dp", "mp"))
    copies = [send("dp", d, mine, mine, s0, r0) for d in range(1, n)]
    invert(system_ref, inverse)
    load.wait()
    tile = rows // 4

    def multiply(index, start):
        def body(t, carry):
            at = rows_of(t, tile)
            value = dot(
                grad[at, columns_of(index, width)], merged_ref[:, columns_of(index, width)], NT
            )
            sums[at, :] = value if start else sums[at, :] + value
            return carry

        lax.fori_loop(0, 4, body, 0)

    multiply(me_dp, True)
    for d in range(1, n):
        copies[d - 1].wait()
        multiply(peer("dp", n - d), False)
    proj[:rows, :] = sums[...].astype(BF16)
    if share * mp > rows:
        proj[rows:, :] = jnp.zeros((share * mp - rows, K), BF16)
    copies = [
        send("mp", d, proj.at[rows_of(peer("mp", d), share)], mp_slots.at[me_mp], s1, r1)
        for d in range(1, mp)
    ]
    mp_slots[me_mp] = proj[rows_of(me_mp, share), :]
    for copy in copies:
        copy.wait()
    solved = dot_split(split(sum_slots(mp_slots)), split(inverse[...]))
    part = solved_ref.at[rows_of(me_mp, share)]
    part[...] = solved.astype(BF16)
    copies = [send("mp", d, part, part, s2, r2) for d in range(1, mp)]
    for copy in copies:
        copy.wait()


def vmem():
    return pl.BlockSpec(memory_space=pltpu.VMEM)


def anywhere():
    return pl.BlockSpec(memory_space=pl.ANY)


def dma(count):
    return pltpu.SemaphoreType.DMA((count,))


def round_up(value, multiple):
    return -(-value // multiple) * multiple


def local(gradient, sketches, start_basis):
    n, mp = lax.axis_size("dp"), lax.axis_size("mp")
    rows, columns = gradient.shape
    width = round_up(-(-columns // n), 128)
    padding = ((0, 0), (0, width * n - columns))
    wide_gradient, wide_sketches = gradient, sketches
    if width * n > columns:
        wide_gradient, wide_sketches = jnp.pad(gradient, padding), jnp.pad(sketches, padding)

    gram_rows = n * (n + 1) // 2 * K
    share = round_up(-(-gram_rows // mp), 16)
    gram_rows = share * mp
    slices, gram = pl.pallas_call(
        functools.partial(gram_kernel, n, mp, width, share),
        out_shape=[
            jax.ShapeDtypeStruct((n * K, width), BF16),
            jax.ShapeDtypeStruct((gram_rows, K), BF16),
        ],
        in_specs=[anywhere()],
        out_specs=[vmem(), vmem()],
        scratch_shapes=[
            pltpu.VMEM((gram_rows, K), BF16),
            pltpu.VMEM((mp, share, K), BF16),
            pltpu.VMEM((n, share, K), BF16),
            pltpu.SemaphoreType.DMA,
            dma(n - 1), dma(n - 1), dma(mp - 1), dma(mp - 1),
            dma(n - 1), dma(n - 1), dma(mp - 1), dma(mp - 1),
        ],
        compiler_params=pltpu.CompilerParams(
            collective_id=0, has_side_effects=True, vmem_limit_bytes=VMEM_LIMIT
        ),
        name="gram",
    )(wide_sketches)

    weights, system = pl.pallas_call(
        functools.partial(merge_kernel, n),
        out_shape=[
            jax.ShapeDtypeStruct((n - 1, K, 2 * K), BF16),
            jax.ShapeDtypeStruct((K, K), F32),
        ],
        in_specs=[vmem(), vmem()],
        out_specs=[vmem(), vmem()],
        scratch_shapes=[
            pltpu.VMEM((n * K, n * K), F32),
            pltpu.VMEM((n * K // 2, n * K // 2), F32),
            pltpu.VMEM((n // 2, K, 2 * K), F32),
        ],
        compiler_params=pltpu.CompilerParams(vmem_limit_bytes=VMEM_LIMIT),
        name="merge",
    )(gram, start_basis.T)

    share = round_up(-(-rows // mp), 16)
    merged, solved = pl.pallas_call(
        functools.partial(solve_kernel, n, mp, width, share, rows),
        out_shape=[
            jax.ShapeDtypeStruct((K, n * width), BF16),
            jax.ShapeDtypeStruct((share * mp, K), BF16),
        ],
        in_specs=[vmem(), vmem(), vmem(), anywhere()],
        out_specs=[vmem(), vmem()],
        scratch_shapes=[
            pltpu.VMEM((rows, n * width), BF16),
            pltpu.VMEM((n // 2 * K, width), BF16),
            pltpu.VMEM((K, K), F32),
            pltpu.VMEM((share * mp, K), BF16),
            pltpu.VMEM((rows, K), F32),
            pltpu.VMEM((mp, share, K), BF16),
            pltpu.SemaphoreType.DMA,
            dma(n - 1), dma(n - 1), dma(mp - 1), dma(mp - 1), dma(mp - 1), dma(mp - 1),
        ],
        compiler_params=pltpu.CompilerParams(
            collective_id=1, has_side_effects=True, vmem_limit_bytes=VMEM_LIMIT
        ),
        name="solve",
    )(weights, system, slices, wide_gradient)
    result = gradient.astype(F32) - jnp.dot(
        solved[:rows], merged[:, :columns], preferred_element_type=F32
    )
    return result.astype(BF16)


def solution(mesh):
    in_specs = (P("dp", "mp"), P("dp", "mp"), P())
    out_specs = P("dp", "mp")
    return jax.shard_map(local, mesh=mesh, in_specs=in_specs, out_specs=out_specs, check_vma=False)
```

time: 556 us -> 284 us (0.51); the launches traced: 550 us -> 284 us
  waiting for transfers between devices: 320 us -> 0 us
  Pallas kernels: 0 us -> 270 us
  matrix products: 141 us -> 12 us
  other arithmetic: 59.7 us -> 0 us
  between operations: 22.9 us -> 0.02 us
    pallas_call x0 -> x3, Pallas kernels: none -> 270 us  [the longest x1 100 us: local(): pl.pallas_call(functools.partial(gram_kernel, n, mp, width, share), out_s...]
    psum x3 -> x0, waiting for transfers between devices: 163 us -> none  [the longest x2 108 us: local(): gram = lax.psum(local_gram.astype(jnp.bfloat16), 'mp').astype(jnp.float32)]
    ppermute x2 -> x0, waiting for transfers between devices: 157 us -> none  [partner_2(): return lax.ppermute(value, axis, pairs)]
    dot_general x113 -> x1, matrix products: 135 us -> 12 us  [local(): jnp.dot(solved[:rows], merged[:, :columns], preferred_element_type=F32)]
    another operation x9 -> x0, other arithmetic: 54.9 us -> none  [the longest x6 34.4 us: solve_rows(): lower = jnp.linalg.cholesky(system)]
    another operation x18 -> x0, local copies, waits for them, and re-layouts: 5.63 us -> none
  transfers between devices with their start and end apart: 5 -> 0, of which waited for: 5 -> 0; matrix products, arithmetic and copies ran while one was open for 0% -> 0% of each run, Pallas kernels for 0% -> 0%
where the time goes in v1:
time: 284 us
  Pallas kernels  270 us (95%)
  matrix products  12 us (4%)
    pallas_call x1, Pallas kernels, local(): pl.pallas_call(functools.partial(gram_kernel, n, mp, width, share), out_s...  100 us
    pallas_call x1, Pallas kernels, local(): pl.pallas_call(functools.partial(merge_kernel, n), out_shape=[jax.ShapeDt...  86.9 us
    pallas_call x1, Pallas kernels, local(): pl.pallas_call(functools.partial(solve_kernel, n, mp, width, share, rows)...  83.3 us
    dot_general x1, matrix products, local(): jnp.dot(solved[:rows], merged[:, :columns], preferred_element_type=F32)  12 us

profile of v1, /device:TPU:25, one launch (start us, length us, event | category | flops | bytes accessed | tf_op | source)
XLA Modules:
  0.0 284.2 jit_solution(16589816838984345727)
XLA Ops:
  0.0 2.0 copy.4
  2.0 100.0 %gram.1 = (bf16[1024,1152]{1,0:T(8,128)(2,1)}, bf16[2560,256]{1,0:T(8,128)(2,1)}) custom-call(bf16[256,4608]{1,0:T(8,128)(2,1)} %sketch_ref.1), custom_call_target="tpu_custom_call" | custom-call | tf_op jit(solution)/shard_map/gram/pallas_call | solution.py:290
  102.0 86.9 %merge.1 = (bf16[3,256,512]{2,1,0:T(8,128)(2,1)}, f32[256,256]{1,0:T(8,128)}) custom-call(bf16[2560,256]{1,0:T(8,128)(2,1)} %get-tuple-element.11.gram_ref, f32[256,512]{1,0:T(8,128)} %bitcast.3), custom_call_target="tpu_custom_call" | custom-call | tf_op jit(solution)/shard_map/merge/pallas_call | solution.py:312
  188.9 83.3 %solve.1 = (bf16[256,4608]{1,0:T(8,128)(2,1)}, bf16[1152,256]{1,0:T(8,128)(2,1)}) custom-call(bf16[3,256,512]{2,1,0:T(8,128)(2,1)} %get-tuple-element.12.weights_ref, f32[256,256]{1,0:T(8,128)} %get-tuple-element.13.system_ref, bf16[1024,1152]{1,0:T(8,128)(2,1)} %get-tuple-element.14.slice_ref, bf16[1152,4608]{1,0:T(8,128)(2,1)} %gradient_ref.1), custom_call_target="tpu_custom_call" | custom-call | tf_op jit(solution)/shard_map/solve/pallas_call | solution.py:330
  272.2 12.0 %fusion = bf16[1152,4608]{1,0:T(8,128)(2,1)} fusion(bf16[1152,256]{1,0:T(8,128)(2,1)} %get-tuple-element.15, bf16[256,4608]{1,0:T(8,128)(2,1)} %get-tuple-element.16, bf16[1152,4608]{1,0:T(8,128)(2,1)} %gradient_ref.1), kind=kOutput, calls=%fused_computation.1 | convolution fusion | flops 2733834240 | bytes 24182784 | tf_op jit(solution)/shard_map/dot_general | solution.py:353

commit v2 on v1

--- a/solution.py
+++ b/solution.py
@@ -13,7 +13,7 @@
 BF16 = jnp.bfloat16
 F32 = jnp.float32
 MESH = pl.DeviceIdType.MESH
-VMEM_LIMIT = 56 * 2**20
+MIB = 2**20
 NN = (((1,), (0,)), ((), ()))
 NT = (((1,), (1,)), ((), ()))
 
@@ -48,6 +48,33 @@
     return copy
 
 
+def core_send(source, target, core, chip, send_sem, recv_sem):
+    copy = pltpu.make_async_remote_copy(
+        src_ref=source,
+        dst_ref=target,
+        send_sem=send_sem,
+        recv_sem=recv_sem,
+        device_id={"mp": 2 * chip + 1 - core},
+        device_id_type=MESH,
+    )
+    copy.start()
+    return copy
+
+
+def chip_send(offset, source, target, core, chip, send_sem, recv_sem):
+    chips = lax.axis_size("mp") // 2
+    copy = pltpu.make_async_remote_copy(
+        src_ref=source,
+        dst_ref=target,
+        send_sem=send_sem.at[offset - 1],
+        recv_sem=recv_sem.at[offset - 1],
+        device_id={"mp": 2 * lax.rem(chip + offset, chips) + core},
+        device_id_type=MESH,
+    )
+    copy.start()
+    return copy
+
+
 def rows_of(index, count):
     return pl.ds(pl.multiple_of(index * count, 16), count)
 
@@ -77,8 +104,9 @@
 
 
 def gram_kernel(
-    n, mp, width, share, sketch_ref, slice_ref, gram_ref, part, mp_slots, dp_slots,
-    local_sem, s0, r0, s1, r1, s2, r2, s3, r3,
+    n, mp, width, share, sketch_ref, basis_ref, slice_ref, gram_ref, turned_ref,
+    part, core_slot, half, mp_slots, dp_slots,
+    local_sem, s0, r0, s1, r1, s2, r2, s3, r3, s4, r4, s5, r5,
 ):
     me_dp, me_mp = lax.axis_index("dp"), lax.axis_index("mp")
     own = pltpu.make_async_copy(
@@ -93,6 +121,7 @@
         )
         for d in range(1, n)
     ]
+    turned_ref[...] = basis_ref[...].T
     own.wait()
     for copy in copies:
         copy.wait()
@@ -103,27 +132,38 @@
                 slice_ref[i * K:(i + 1) * K, :], slice_ref[j * K:(j + 1) * K, :], NT
             ).astype(BF16)
             block += 1
+    chips = mp // 2
+    core, chip = lax.rem(me_mp, 2), me_mp // 2
+    twin = 1 - core
+    copy = core_send(part.at[rows_of(twin, chips * share)], core_slot, core, chip, s1, r1)
+    copy.wait()
+    half[...] = (
+        part[rows_of(core, chips * share), :].astype(F32) + core_slot[...].astype(F32)
+    ).astype(BF16)
     copies = [
-        send("mp", d, part.at[rows_of(peer("mp", d), share)], mp_slots.at[me_mp], s1, r1)
-        for d in range(1, mp)
+        chip_send(d, half.at[rows_of(lax.rem(chip + d, chips), share)], mp_slots.at[chip], core, chip, s2, r2)
+        for d in range(1, chips)
     ]
-    mp_slots[me_mp] = part[rows_of(me_mp, share), :]
+    mp_slots[chip] = half[rows_of(chip, share), :]
     for copy in copies:
         copy.wait()
     dp_slots[me_dp] = sum_slots(mp_slots).astype(BF16)
     copies = [
-        send("dp", d, dp_slots.at[me_dp], dp_slots.at[me_dp], s2, r2) for d in range(1, n)
+        send("dp", d, dp_slots.at[me_dp], dp_slots.at[me_dp], s3, r3) for d in range(1, n)
     ]
     for copy in copies:
         copy.wait()
-    mine = gram_ref.at[rows_of(me_mp, share)]
+    mine = gram_ref.at[rows_of(core * chips + chip, share)]
     mine[...] = sum_slots(dp_slots).astype(BF16)
-    copies = [send("mp", d, mine, mine, s3, r3) for d in range(1, mp)]
-    for copy in copies:
-        copy.wait()
-
-
-def merge_kernel(n, gram_ref, basis_ref, weights_ref, system_ref, full, following, basis):
+    copies = [chip_send(d, mine, mine, core, chip, s4, r4) for d in range(1, chips)]
+    for copy in copies:
+        copy.wait()
+    mine = gram_ref.at[rows_of(core, chips * share)]
+    copy = core_send(mine, mine, core, chip, s5, r5)
+    copy.wait()
+
+
+def merge_kernel(n, gram_ref, basis_ref, weights_ref, system_ref, full, following, basis, fine):
     block = 0
     for i in range(n):
         for j in range(i, n):
@@ -139,25 +179,33 @@
         sides = [slice(2 * K * p, 2 * K * (p + 1)) for p in range(pairs)]
         for p in range(pairs):
             basis[p] = basis_ref[...]
+            fine[2 * p], fine[2 * p + 1] = split(source[sides[p], sides[p]])
+
+        def multiply(value, p):
+            high, low = split(value)
+            image = dot(high, fine[2 * p]) + dot(low, fine[2 * p])
+            if blocks == n:
+                return image
+            return image + dot(high, fine[2 * p + 1])
 
         def newton_schulz(step, carry):
             for p in range(pairs):
                 value = basis[p]
-                parts = split(value)
-                square = split(dot_split(parts, parts, NT))
-                basis[p] = 1.5 * value - 0.5 * dot_split(square, parts)
+                short = value.astype(BF16)
+                square = dot(short, short, NT).astype(BF16)
+                basis[p] = 1.5 * value - 0.5 * dot(square, short)
             return carry
 
         def iteration(step, carry):
             for p in range(pairs):
-                image = dot_split(split(basis[p]), split(source[sides[p], sides[p]]))
+                image = multiply(basis[p], p)
                 basis[p] = image / jnp.sqrt(jnp.sum(image * image) + 1e-06)
             return lax.fori_loop(0, NS_STEPS, newton_schulz, carry)
 
         lax.fori_loop(0, ITERS, iteration, 0)
         for p in range(pairs):
             value = basis[p]
-            image = dot_split(split(value), split(source[sides[p], sides[p]]))
+            image = multiply(value, p)
             energy = jnp.sum(value * image, axis=1, keepdims=True)
             shrink = 0.5 * jnp.min(energy)
             factor = jnp.sqrt(1.0 - shrink / energy)
@@ -203,7 +251,7 @@
 def solve_kernel(
     n, mp, width, share, rows, weights_ref, system_ref, slice_ref, gradient_ref,
     merged_ref, solved_ref, grad, level, inverse, proj, sums, mp_slots,
-    local_sem, s0, r0, s1, r1, s2, r2,
+    local_sem, s0, r0, s1, r1, s2, r2, s3, r3,
 ):
     me_dp, me_mp = lax.axis_index("dp"), lax.axis_index("mp")
     load = pltpu.make_async_copy(gradient_ref, grad, local_sem)
@@ -221,7 +269,28 @@
         source = level
         first += blocks
     greet(("dp", "mp"))
-    copies = [send("dp", d, mine, mine, s0, r0) for d in range(1, n)]
+    def pass_on(index, offset, semaphores):
+        part = merged_ref.at[:, columns_of(index, width)]
+        at = lax.rem(index + n, n)
+        return pltpu.make_async_remote_copy(
+            src_ref=part,
+            dst_ref=part,
+            send_sem=semaphores[0].at[at],
+            recv_sem=semaphores[1].at[at],
+            device_id={"dp": lax.rem(me_dp + offset + n, n)},
+            device_id_type=MESH,
+        )
+
+    up, down = (s0, r0), (s3, r3)
+
+    @pl.when(me_dp < n - 1)
+    def _():
+        pass_on(me_dp, 1, up).start()
+
+    @pl.when(me_dp > 0)
+    def _():
+        pass_on(me_dp, -1, down).start()
+
     invert(system_ref, inverse)
     load.wait()
     tile = rows // 4
@@ -239,8 +308,42 @@
 
     multiply(me_dp, True)
     for d in range(1, n):
-        copies[d - 1].wait()
-        multiply(peer("dp", n - d), False)
+        below, above = me_dp - d, me_dp + d
+
+        @pl.when(below >= 0)
+        def _():
+            pass_on(below, 1, up).wait_recv()
+
+        @pl.when((below >= 0) & (me_dp < n - 1))
+        def _():
+            pass_on(below, 1, up).start()
+
+        @pl.when(above < n)
+        def _():
+            pass_on(above, -1, down).wait_recv()
+
+        @pl.when((above < n) & (me_dp > 0))
+        def _():
+            pass_on(above, -1, down).start()
+
+        @pl.when(below >= 0)
+        def _():
+            multiply(below, False)
+
+        @pl.when(above < n)
+        def _():
+            multiply(above, False)
+
+    for d in range(n):
+
+        @pl.when((me_dp - d >= 0) & (me_dp < n - 1))
+        def _():
+            pass_on(me_dp - d, 1, up).wait_send()
+
+        @pl.when((me_dp + d < n) & (me_dp > 0))
+        def _():
+            pass_on(me_dp + d, -1, down).wait_send()
+
     proj[:rows, :] = sums[...].astype(BF16)
     if share * mp > rows:
         proj[rows:, :] = jnp.zeros((share * mp - rows, K), BF16)
@@ -259,6 +362,11 @@
         copy.wait()
 
 
+def subtract_kernel(gradient_ref, solved_ref, merged_ref, result_ref):
+    result = gradient_ref[...].astype(F32) - dot(solved_ref[...], merged_ref[...])
+    result_ref[...] = result.astype(BF16)
+
+
 def vmem():
     return pl.BlockSpec(memory_space=pltpu.VMEM)
 
@@ -287,27 +395,30 @@
     gram_rows = n * (n + 1) // 2 * K
     share = round_up(-(-gram_rows // mp), 16)
     gram_rows = share * mp
-    slices, gram = pl.pallas_call(
+    one = pltpu.SemaphoreType.DMA
+    slices, gram, turned = pl.pallas_call(
         functools.partial(gram_kernel, n, mp, width, share),
         out_shape=[
             jax.ShapeDtypeStruct((n * K, width), BF16),
             jax.ShapeDtypeStruct((gram_rows, K), BF16),
-        ],
-        in_specs=[anywhere()],
-        out_specs=[vmem(), vmem()],
+            jax.ShapeDtypeStruct((K, 2 * K), F32),
+        ],
+        in_specs=[anywhere(), vmem()],
+        out_specs=[vmem(), vmem(), vmem()],
         scratch_shapes=[
             pltpu.VMEM((gram_rows, K), BF16),
-            pltpu.VMEM((mp, share, K), BF16),
+            pltpu.VMEM((gram_rows // 2, K), BF16),
+            pltpu.VMEM((gram_rows // 2, K), BF16),
+            pltpu.VMEM((mp // 2, share, K), BF16),
             pltpu.VMEM((n, share, K), BF16),
-            pltpu.SemaphoreType.DMA,
-            dma(n - 1), dma(n - 1), dma(mp - 1), dma(mp - 1),
-            dma(n - 1), dma(n - 1), dma(mp - 1), dma(mp - 1),
+            one, dma(n - 1), dma(n - 1), one, one, dma(mp // 2 - 1), dma(mp // 2 - 1),
+            dma(n - 1), dma(n - 1), dma(mp // 2 - 1), dma(mp // 2 - 1), one, one,
         ],
         compiler_params=pltpu.CompilerParams(
-            collective_id=0, has_side_effects=True, vmem_limit_bytes=VMEM_LIMIT
+            collective_id=0, has_side_effects=True, vmem_limit_bytes=MIB * 16 + 8 * gram_rows * K
         ),
         name="gram",
-    )(wide_sketches)
+    )(wide_sketches, start_basis)
 
     weights, system = pl.pallas_call(
         functools.partial(merge_kernel, n),
@@ -321,10 +432,11 @@
             pltpu.VMEM((n * K, n * K), F32),
             pltpu.VMEM((n * K // 2, n * K // 2), F32),
             pltpu.VMEM((n // 2, K, 2 * K), F32),
-        ],
-        compiler_params=pltpu.CompilerParams(vmem_limit_bytes=VMEM_LIMIT),
+            pltpu.VMEM((n, 2 * K, 2 * K), BF16),
+        ],
+        compiler_params=pltpu.CompilerParams(vmem_limit_bytes=MIB * 16 + 8 * (n * K) ** 2),
         name="merge",
-    )(gram, start_basis.T)
+    )(gram, turned)
 
     share = round_up(-(-rows // mp), 16)
     merged, solved = pl.pallas_call(
@@ -342,18 +454,27 @@
             pltpu.VMEM((share * mp, K), BF16),
             pltpu.VMEM((rows, K), F32),
             pltpu.VMEM((mp, share, K), BF16),
-            pltpu.SemaphoreType.DMA,
-            dma(n - 1), dma(n - 1), dma(mp - 1), dma(mp - 1), dma(mp - 1), dma(mp - 1),
+            one, dma(n), dma(n), dma(mp - 1), dma(mp - 1), dma(mp - 1), dma(mp - 1), dma(n), dma(n),
         ],
         compiler_params=pltpu.CompilerParams(
-            collective_id=1, has_side_effects=True, vmem_limit_bytes=VMEM_LIMIT
+            collective_id=1, has_side_effects=True, vmem_limit_bytes=MIB * 20 + 2 * rows * n * width
         ),
         name="solve",
     )(weights, system, slices, wide_gradient)
-    result = gradient.astype(F32) - jnp.dot(
-        solved[:rows], merged[:, :columns], preferred_element_type=F32
-    )
-    return result.astype(BF16)
+    tile = rows // 8 if rows % 128 == 0 else rows
+    return pl.pallas_call(
+        subtract_kernel,
+        out_shape=jax.ShapeDtypeStruct((rows, columns), BF16),
+        grid=(rows // tile,),
+        in_specs=[
+            pl.BlockSpec((tile, columns), lambda i: (i, 0)),
+            pl.BlockSpec((tile, K), lambda i: (i, 0)),
+            pl.BlockSpec((K, columns), lambda i: (0, 0)),
+        ],
+        out_specs=pl.BlockSpec((tile, columns), lambda i: (i, 0)),
+        compiler_params=pltpu.CompilerParams(vmem_limit_bytes=MIB * 24),
+        name="subtract",
+    )(gradient, solved[:rows], merged[:, :columns])
 
 
 def solution(mesh):

time: 284 us -> 217 us (0.76); the launches traced: 284 us -> 213 us
  Pallas kernels: 270 us -> 207 us
  matrix products: 12 us -> 0 us
  local copies, waits for them, and re-layouts: 2.04 us -> 6.72 us
    pallas_call x1, Pallas kernels: 86.9 us -> 44.2 us  [local(): pl.pallas_call(functools.partial(merge_kernel, n), out_shape=[jax.ShapeDt...]
    pallas_call x1, Pallas kernels: 83.3 us -> 65.8 us  [local(): pl.pallas_call(functools.partial(solve_kernel, n, mp, width, share, rows)...]
    dot_general x1 -> x0, matrix products: 12 us -> none  [local(): jnp.dot(solved[:rows], merged[:, :columns], preferred_element_type=F32)]
    pallas_call x1, Pallas kernels: 100 us -> 89.6 us  [local(): pl.pallas_call(functools.partial(gram_kernel, n, mp, width, share), out_s...]
    pallas_call x0 -> x1, Pallas kernels: none -> 6.88 us  [local(): pl.pallas_call(subtract_kernel, out_shape=jax.ShapeDtypeStruct((rows, col...]
    unnamed x1 -> x8, local copies, waits for them, and re-layouts: 2.04 us -> 6.72 us
where the time goes in v2:
time: 217 us; the launch traced here: 213 us
  Pallas kernels  207 us (95%)
  local copies, waits for them, and re-layouts  6.72 us (3%)
    pallas_call x1, Pallas kernels, local(): pl.pallas_call(functools.partial(gram_kernel, n, mp, width, share), out_s...  89.6 us
    pallas_call x1, Pallas kernels, local(): pl.pallas_call(functools.partial(solve_kernel, n, mp, width, share, rows)...  65.8 us
    pallas_call x1, Pallas kernels, local(): pl.pallas_call(functools.partial(merge_kernel, n), out_shape=[jax.ShapeDt...  44.2 us
    pallas_call x1, Pallas kernels, local(): pl.pallas_call(subtract_kernel, out_shape=jax.ShapeDtypeStruct((rows, col...  6.88 us
    unnamed x8, local copies, waits for them, and re-layouts  6.72 us

profile of v2, /device:TPU:25, one launch (start us, length us, event | category | flops | bytes accessed | tf_op | source)
XLA Modules:
  0.0 213.3 jit_solution(16818044617889773598)
XLA Ops:
  0.0 0.0 copy-start.2
  0.0 1.7 copy-done.2
  1.7 0.0 copy-start.3
  1.7 1.0 copy-done.3
  2.7 89.6 %gram.1 = (bf16[1024,1152]{1,0:T(8,128)(2,1)S(1)}, bf16[2560,256]{1,0:T(8,128)(2,1)S(1)}, f32[256,512]{1,0:T(8,128)S(1)}) custom-call(bf16[256,4608]{1,0:T(8,128)(2,1)S(1)} %copy-done.2, f32[512,256]{1,0:T(8,128)S(1)} %copy-done.3), custom_call_target="tpu_custom_call" | custom-call | tf_op jit(solution)/shard_map/gram/pallas_call | solution.py:399
  92.3 44.2 %merge.1 = (bf16[3,256,512]{2,1,0:T(8,128)(2,1)S(1)}, f32[256,256]{1,0:T(8,128)S(1)}) custom-call(bf16[2560,256]{1,0:T(8,128)(2,1)S(1)} %get-tuple-element.12.gram_ref, f32[256,512]{1,0:T(8,128)S(1)} %get-tuple-element.13.basis_ref), custom_call_target="tpu_custom_call" | custom-call | tf_op jit(solution)/shard_map/merge/pallas_call | solution.py:423
  136.5 0.0 copy-start
  136.5 4.0 %copy-done = bf16[1152,4608]{1,0:T(8,128)(2,1)S(1)} copy-done((bf16[1152,4608]{1,0:T(8,128)(2,1)S(1)}, bf16[1152,4608]{1,0:T(8,128)(2,1)}, u32[]{:S(2)}) %copy-start) | copy-done | bytes 10616856
  140.5 0.0 copy-start.1
  140.5 65.8 %solve.1 = (bf16[256,4608]{1,0:T(8,128)(2,1)S(1)}, bf16[1152,256]{1,0:T(8,128)(2,1)S(1)}) custom-call(bf16[3,256,512]{2,1,0:T(8,128)(2,1)S(1)} %get-tuple-element.14.weights_ref, f32[256,256]{1,0:T(8,128)S(1)} %get-tuple-element.15.system_ref, bf16[1024,1152]{1,0:T(8,128)(2,1)S(1)} %get-tuple-element.16.slice_ref, bf16[1152,4608]{1,0:T(8,128)(2,1)S(1)} %copy-done), custom_call_target="tpu_custom_call" | custom-call | tf_op jit(solution)/shard_map/solve/pallas_call | solution.py:442
  206.4 0.0 copy-done.1
  206.4 6.9 %subtract.1 = bf16[1152,4608]{1,0:T(8,128)(2,1)} custom-call(bf16[1152,4608]{1,0:T(8,128)(2,1)S(1)} %copy-done.1, bf16[1152,256]{1,0:T(8,128)(2,1)S(1)} %get-tuple-element.17.solved_ref, bf16[256,4608]{1,0:T(8,128)(2,1)S(1)} %get-tuple-element.18.merged_ref), custom_call_target="tpu_custom_call" | custom-call | tf_op jit(solution)/shard_map/subtract/pallas_call | solution.py:465
Async XLA Ops:
  0.0 1.7 copy-start.2
  1.7 1.0 copy-start.3
  136.5 4.0 %copy-start = (bf16[1152,4608]{1,0:T(8,128)(2,1)S(1)}, bf16[1152,4608]{1,0:T(8,128)(2,1)}, u32[]{:S(2)}) copy-start(bf16[1152,4608]{1,0:T(8,128)(2,1)} %gradient_ref.3) | copy-start | bytes 31850500
  140.5 65.8 %copy-start.1 = (bf16[1152,4608]{1,0:T(8,128)(2,1)S(1)}, bf16[1152,4608]{1,0:T(8,128)(2,1)}, u32[]{:S(2)}) copy-start(bf16[1152,4608]{1,0:T(8,128)(2,1)} %gradient_ref.3) | copy-start | bytes 31850500

commit v3 on v2

--- a/solution.py
+++ b/solution.py
@@ -105,8 +105,8 @@
 
 def gram_kernel(
     n, mp, width, share, sketch_ref, basis_ref, slice_ref, gram_ref, turned_ref,
-    part, core_slot, half, mp_slots, dp_slots,
-    local_sem, s0, r0, s1, r1, s2, r2, s3, r3, s4, r4, s5, r5,
+    part, core_slot, half, mp_slots, plane, dp_slots,
+    local_sem, s0, r0, s1, r1, s2, r2, s3, r3, s4, r4, s5, r5, s6, r6,
 ):
     me_dp, me_mp = lax.axis_index("dp"), lax.axis_index("mp")
     own = pltpu.make_async_copy(
@@ -147,14 +147,21 @@
     mp_slots[chip] = half[rows_of(chip, share), :]
     for copy in copies:
         copy.wait()
-    dp_slots[me_dp] = sum_slots(mp_slots).astype(BF16)
+    plane[...] = sum_slots(mp_slots).astype(BF16)
+    fourth = share // n
     copies = [
-        send("dp", d, dp_slots.at[me_dp], dp_slots.at[me_dp], s3, r3) for d in range(1, n)
+        send("dp", d, plane.at[rows_of(peer("dp", d), fourth)], dp_slots.at[me_dp], s3, r3)
+        for d in range(1, n)
     ]
+    dp_slots[me_dp] = plane[rows_of(me_dp, fourth), :]
+    for copy in copies:
+        copy.wait()
+    mine = gram_ref.at[rows_of((core * chips + chip) * n + me_dp, fourth)]
+    mine[...] = sum_slots(dp_slots).astype(BF16)
+    copies = [send("dp", d, mine, mine, s6, r6) for d in range(1, n)]
     for copy in copies:
         copy.wait()
     mine = gram_ref.at[rows_of(core * chips + chip, share)]
-    mine[...] = sum_slots(dp_slots).astype(BF16)
     copies = [chip_send(d, mine, mine, core, chip, s4, r4) for d in range(1, chips)]
     for copy in copies:
         copy.wait()
@@ -200,7 +207,7 @@
             for p in range(pairs):
                 image = multiply(basis[p], p)
                 basis[p] = image / jnp.sqrt(jnp.sum(image * image) + 1e-06)
-            return lax.fori_loop(0, NS_STEPS, newton_schulz, carry)
+            return lax.fori_loop(0, NS_STEPS, newton_schulz, carry, unroll=True)
 
         lax.fori_loop(0, ITERS, iteration, 0)
         for p in range(pairs):
@@ -393,7 +400,7 @@
         wide_gradient, wide_sketches = jnp.pad(gradient, padding), jnp.pad(sketches, padding)
 
     gram_rows = n * (n + 1) // 2 * K
-    share = round_up(-(-gram_rows // mp), 16)
+    share = round_up(-(-gram_rows // mp), 16 * n)
     gram_rows = share * mp
     one = pltpu.SemaphoreType.DMA
     slices, gram, turned = pl.pallas_call(
@@ -410,12 +417,17 @@
             pltpu.VMEM((gram_rows // 2, K), BF16),
             pltpu.VMEM((gram_rows // 2, K), BF16),
             pltpu.VMEM((mp // 2, share, K), BF16),
-            pltpu.VMEM((n, share, K), BF16),
+            pltpu.VMEM((share, K), BF16),
+            pltpu.VMEM((n, share // n, K), BF16),
             one, dma(n - 1), dma(n - 1), one, one, dma(mp // 2 - 1), dma(mp // 2 - 1),
             dma(n - 1), dma(n - 1), dma(mp // 2 - 1), dma(mp // 2 - 1), one, one,
+            dma(n - 1), dma(n - 1),
         ],
         compiler_params=pltpu.CompilerParams(
             collective_id=0, has_side_effects=True, vmem_limit_bytes=MIB * 16 + 8 * gram_rows * K
+        ),
+        cost_estimate=pl.CostEstimate(
+            flops=60 * 10**9, bytes_accessed=2 * 10**8, transcendentals=0
         ),
         name="gram",
     )(wide_sketches, start_basis)
@@ -435,6 +447,9 @@
             pltpu.VMEM((n, 2 * K, 2 * K), BF16),
         ],
         compiler_params=pltpu.CompilerParams(vmem_limit_bytes=MIB * 16 + 8 * (n * K) ** 2),
+        cost_estimate=pl.CostEstimate(
+            flops=40 * 10**9, bytes_accessed=10**8, transcendentals=0
+        ),
         name="merge",
     )(gram, turned)
 

time: 217 us -> 194 us (0.89)
  Pallas kernels: 207 us -> 188 us
  local copies, waits for them, and re-layouts: 6.72 us -> 2.72 us
    pallas_call x1, Pallas kernels: 44.2 us -> 31.6 us  [local(): pl.pallas_call(functools.partial(merge_kernel, n), out_shape=[jax.ShapeDt...]
    unnamed x8 -> x10, local copies, waits for them, and re-layouts: 6.72 us -> 2.72 us
    pallas_call x1, Pallas kernels: 89.6 us -> 86.4 us  [local(): pl.pallas_call(functools.partial(gram_kernel, n, mp, width, share), out_s...]
    pallas_call x1, Pallas kernels: 65.8 us -> 63.2 us  [local(): pl.pallas_call(functools.partial(solve_kernel, n, mp, width, share, rows)...]
where the time goes in v3:
time: 194 us; the launch traced here: 191 us
  Pallas kernels  188 us (97%)
  local copies, waits for them, and re-layouts  2.72 us (1%)
    pallas_call x1, Pallas kernels, local(): pl.pallas_call(functools.partial(gram_kernel, n, mp, width, share), out_s...  86.4 us
    pallas_call x1, Pallas kernels, local(): pl.pallas_call(functools.partial(solve_kernel, n, mp, width, share, rows)...  63.2 us
    pallas_call x1, Pallas kernels, local(): pl.pallas_call(functools.partial(merge_kernel, n), out_shape=[jax.ShapeDt...  31.6 us
    pallas_call x1, Pallas kernels, local(): pl.pallas_call(subtract_kernel, out_shape=jax.ShapeDtypeStruct((rows, col...  6.87 us

profile of v3, /device:TPU:25, one launch (start us, length us, event | category | flops | bytes accessed | tf_op | source)
XLA Modules:
  0.0 190.9 jit_solution(17399961132399501918)
XLA Ops:
  0.0 0.0 copy-start
  0.0 1.7 copy-done
  1.7 0.0 copy-start.1
  1.7 1.0 copy-done.1
  2.7 86.4 %gram.1 = (bf16[1024,1152]{1,0:T(8,128)(2,1)S(1)}, bf16[2560,256]{1,0:T(8,128)(2,1)S(1)}, f32[256,512]{1,0:T(8,128)S(1)}) custom-call(bf16[256,4608]{1,0:T(8,128)(2,1)S(1)} %copy-done, f32[512,256]{1,0:T(8,128)S(1)} %copy-done.1), custom_call_target="tpu_custom_call" | custom-call | flops 60000002048 | bytes 200000000 | tf_op jit(solution)/shard_map/gram/pallas_call | solution.py:406
  89.1 0.0 slice-start
  89.1 0.0 slice-start.1
  89.2 0.0 slice-start.2
  89.2 31.6 %merge.1 = (bf16[3,256,512]{2,1,0:T(8,128)(2,1)S(1)}, f32[256,256]{1,0:T(8,128)S(1)}) custom-call(bf16[2560,256]{1,0:T(8,128)(2,1)S(1)} %get-tuple-element.12.gram_ref, f32[256,512]{1,0:T(8,128)S(1)} %get-tuple-element.13.basis_ref), custom_call_target="tpu_custom_call" | custom-call | flops 40000000000 | bytes 100000000 | tf_op jit(solution)/shard_map/merge/pallas_call | solution.py:435
  120.7 0.0 slice-done
  120.8 0.0 slice-done.1
  120.8 0.0 slice-done.2
  120.8 63.2 %solve.1 = (bf16[256,4608]{1,0:T(8,128)(2,1)S(1)}, bf16[1152,256]{1,0:T(8,128)(2,1)S(1)}) custom-call(bf16[3,256,512]{2,1,0:T(8,128)(2,1)S(1)} %get-tuple-element.14.weights_ref, f32[256,256]{1,0:T(8,128)S(1)} %get-tuple-element.15.system_ref, bf16[1024,1152]{1,0:T(8,128)(2,1)S(1)} %get-tuple-element.16.slice_ref, bf16[1152,4608]{1,0:T(8,128)(2,1)S(1)} %bitcast.1), custom_call_target="tpu_custom_call" | custom-call | tf_op jit(solution)/shard_map/solve/pallas_call | solution.py:457
  184.0 6.9 %subtract.1 = bf16[1152,4608]{1,0:T(8,128)(2,1)} custom-call(bf16[1152,4608]{1,0:T(8,128)(2,1)S(1)} %bitcast.1, bf16[1152,256]{1,0:T(8,128)(2,1)S(1)} %get-tuple-element.17.solved_ref, bf16[256,4608]{1,0:T(8,128)(2,1)S(1)} %get-tuple-element.18.merged_ref), custom_call_target="tpu_custom_call" | custom-call | tf_op jit(solution)/shard_map/subtract/pallas_call | solution.py:480
  (1 shorter events, 0.0 us)
Async XLA Ops:
  0.0 1.7 copy-start
  1.7 1.0 copy-start.1
  89.1 31.6 %slice-start = ((s8[10616832]{0:T(1024)(128)(4,1)}), s8[4194304]{0:T(1024)(128)(4,1)S(1)}, s32[]{:S(2)}) async-start(s8[10616832]{0:T(1024)(128)(4,1)} %bitcast), calls=%async_computation | async-start | bytes 8388608
  89.1 31.6 %slice-start.1 = ((s8[10616832]{0:T(1024)(128)(4,1)}), s8[4194304]{0:T(1024)(128)(4,1)S(1)}, s32[]{:S(2)}) async-start(s8[10616832]{0:T(1024)(128)(4,1)} %bitcast), calls=%async_computation.1 | async-start | bytes 8388608
  89.2 31.6 %slice-start.2 = ((s8[10616832]{0:T(1024)(128)(4,1)}), s8[2228224]{0:T(1024)(128)(4,1)S(1)}, s32[]{:S(2)}) async-start(s8[10616832]{0:T(1024)(128)(4,1)} %bitcast), calls=%async_computation.2 | async-start | bytes 4456448
